TPU v7x, 128 devices: a whole 4x4x4 slice. The times are simulated.
128 devices in a mesh: rep: 4 (over z_hi, core), fsdp: 32 (over z_lo, x, y).
Axes of the slice: x: 4, y: 4, z: 4 (z_hi: 2, z_lo: 2; z = z_hi * 2 + z_lo), core: 2. Of those that a mesh axis runs over, the one named last changes fastest.
Arguments:
- in_table: bfloat16 [4, 256, 2048], P('rep'), may hold values from -6 to 6
- target_table: bfloat16 [4, 256, 2048], P('rep'), may hold values from -3 to 3
- in_ids: int32 [4, 4, 256], P('rep'), may hold values from 0 to 255
- target_ids: int32 [4, 4, 256], P('rep'), may hold values from 0 to 255
- gate_up: float32 [2, 2048, 14336], P(None, 'rep', 'fsdp'), may hold values from -6 to 6
- down: float32 [14336, 2048], P('fsdp', 'rep'), may hold values from -6 to 6
- mom_gate_up: float32 [2, 2048, 14336], P(None, 'rep', 'fsdp'), may hold values from -0.6 to 0.6
- mom_down: float32 [14336, 2048], P('fsdp', 'rep'), may hold values from -0.6 to 0.6
- m_gate_up: bfloat16 [4, 2, 2048, 14336], P('rep', None, None, 'fsdp'), may hold values from -0.00059890747 to 0.00059890747
- v_gate_up: bfloat16 [4, 2, 2048, 14336], P('rep', None, None, 'fsdp'), may hold values from 9.968062e-10 to 9.9651515e-08
- m_down: bfloat16 [4, 14336, 2048], P('rep', 'fsdp'), may hold values from -0.00059890747 to 0.00059890747
- v_down: bfloat16 [4, 14336, 2048], P('rep', 'fsdp'), may hold values from 9.968062e-10 to 9.9651515e-08
Outputs:
- new_gate_up: float32 [2, 2048, 14336], P(None, 'rep', 'fsdp')
- new_down: float32 [14336, 2048], P('fsdp', 'rep')
- new_mom_gate_up: float32 [2, 2048, 14336], P(None, 'rep', 'fsdp')
- new_mom_down: float32 [14336, 2048], P('fsdp', 'rep')
All inputs are finite; a program needn't handle non-finite values.
Results may differ from a plain program's by a relative error of at most 0.006.
Values may be sent and summed in bfloat16 or wider, within the bound.
A program may use at most 192 MiB of HBM per device.

v0:
```python
import jax
import jax.numpy as jnp
from jax import lax
from jax.sharding import PartitionSpec as P

D = 2048
FF = 14336
STEPS = 4


beta_one = 0.9
beta_two = 0.95
inner_rate = 0.03
decay_rate = 0.1
epsilon = 1e-08
outer_rate = 0.7
momentum_rate = 0.9


def adam_update(weight, grad, first, second):
    first = beta_one * first + (1.0 - beta_one) * grad
    second = beta_two * second + (1.0 - beta_two) * grad * grad
    weight = weight - inner_rate * (first / (jnp.sqrt(second) + epsilon) + decay_rate * weight)
    return (weight, first, second)


def rounded(value):
    narrow = value.astype(jnp.bfloat16)
    narrow = lax.optimization_barrier(narrow)
    return narrow.astype(jnp.float32)


def on_device(
    in_table,
    target_table,
    in_ids,
    target_ids,
    gate_up,
    down,
    mom_gate_up,
    mom_down,
    m_gate_up,
    v_gate_up,
    m_down,
    v_down,
):
    in_scale = 1.0 / D**0.5
    out_scale = 1.0 / FF**0.5
    start_gu, start_down = (
        lax.all_gather(gate_up, "rep", axis=1, tiled=True),
        lax.all_gather(down, "rep", axis=1, tiled=True),
    )
    shards = lax.axis_size("fsdp")
    tokens = in_ids.shape[2]
    row_count = tokens // shards
    table = in_table[0]
    targets = target_table[0]
    weight_gu = start_gu
    weight_down = start_down
    first_gu = m_gate_up[0].astype(jnp.float32)
    second_gu = v_gate_up[0].astype(jnp.float32)
    first_down = m_down[0].astype(jnp.float32)
    second_down = v_down[0].astype(jnp.float32)
    for step in range(STEPS):
        inputs = jnp.take(table, in_ids[0, step], axis=0)
        gu_b = weight_gu.astype(jnp.bfloat16)
        down_b = weight_down.astype(jnp.bfloat16)
        gate = jnp.dot(inputs, gu_b[0], preferred_element_type=jnp.float32) * in_scale
        upper = jnp.dot(inputs, gu_b[1], preferred_element_type=jnp.float32) * in_scale
        hidden = (jax.nn.silu(gate) * upper).astype(jnp.bfloat16)
        own_rows = lax.psum_scatter(
            jnp.dot(hidden, down_b, preferred_element_type=jnp.float32) * out_scale,
            "fsdp",
            scatter_dimension=0,
            tiled=True,
        )
        own_ids = lax.dynamic_slice_in_dim(
            target_ids[0, step], lax.axis_index("fsdp") * row_count, row_count, 0
        )
        wanted = jnp.take(targets, own_ids, axis=0)
        own_grad = ((own_rows - wanted.astype(jnp.float32)) / tokens).astype(jnp.bfloat16)
        out_grad = lax.all_gather(own_grad, "fsdp", axis=0, tiled=True)
        grad_down = (
            lax.dot_general(
                hidden, out_grad, (((0,), (0,)), ((), ())), preferred_element_type=jnp.float32
            )
            * out_scale
        )
        hidden_grad = (
            lax.dot_general(
                out_grad, down_b, (((1,), (1,)), ((), ())), preferred_element_type=jnp.float32
            )
            * out_scale
        )
        sigmoid_gate = jax.nn.sigmoid(gate)
        slope = sigmoid_gate * (1.0 + gate * (1.0 - sigmoid_gate))
        pre_grad = jnp.stack([hidden_grad * upper * slope, hidden_grad * jax.nn.silu(gate)]).astype(
            jnp.bfloat16
        )
        grad_gu = (
            jnp.einsum("td,ktf->kdf", inputs, pre_grad, preferred_element_type=jnp.float32)
            * in_scale
        )
        weight_gu, first_gu, second_gu = adam_update(weight_gu, grad_gu, first_gu, second_gu)
        weight_down, first_down, second_down = adam_update(
            weight_down, grad_down, first_down, second_down
        )
    delta_gu = rounded(start_gu - weight_gu)
    delta_down = rounded(start_down - weight_down)
    total_gu, total_down = (
        lax.psum_scatter(
            delta_gu.astype(jnp.bfloat16), "rep", scatter_dimension=1, tiled=True
        ).astype(jnp.float32),
        lax.psum_scatter(
            delta_down.astype(jnp.bfloat16), "rep", scatter_dimension=1, tiled=True
        ).astype(jnp.float32),
    )
    replicas = lax.axis_size("rep")
    mean_gu = total_gu / replicas
    mean_down = total_down / replicas
    new_mom_gu = momentum_rate * mom_gate_up + mean_gu
    new_mom_down = momentum_rate * mom_down + mean_down
    new_gu = gate_up - outer_rate * (mean_gu + momentum_rate * new_mom_gu)
    new_down = down - outer_rate * (mean_down + momentum_rate * new_mom_down)
    return (new_gu, new_down, new_mom_gu, new_mom_down)


def solution(mesh):
    in_specs = (
        P("rep", None, None),
        P("rep", None, None),
        P("rep", None, None),
        P("rep", None, None),
        P(None, "rep", "fsdp"),
        P("fsdp", "rep"),
        P(None, "rep", "fsdp"),
        P("fsdp", "rep"),
        P("rep", None, None, "fsdp"),
        P("rep", None, None, "fsdp"),
        P("rep", "fsdp", None),
        P("rep", "fsdp", None),
    )
    out_specs = (P(None, "rep", "fsdp"), P("fsdp", "rep"), P(None, "rep", "fsdp"), P("fsdp", "rep"))
    return jax.shard_map(
        on_device, mesh=mesh, in_specs=in_specs, out_specs=out_specs, check_vma=False
    )
```

profile of v0, /device:TPU:1, one launch (start us, length us, event | category | flops | bytes accessed | tf_op | source)
XLA Modules:
  0.0 1568.9 jit_solution(6781261652645693697)
XLA Ops:
  9.6 1.4 gather_fusion
  11.0 58.9 %all-gather.7.cloned.1.call-done = f32[2,2048,448]{1,2,0:T(8,128)} async-done(((f32[2,512,448]{1,2,0:T(8,128)}), f32[2,2048,448]{1,2,0:T(8,128)}) %all-gather.7.cloned.1.call-update) | async-done | bytes 7340048 | tf_op jit(solution)/shard_map/all_gather | solution.py:50
  69.9 3.6 convert_element_type.97
  75.1 1.5 multiply_convert_fusion.11
  76.6 29.9 %all-gather.9.cloned.1.call-done = f32[448,2048]{1,0:T(8,128)} async-done(((f32[448,512]{1,0:T(8,128)}), f32[448,2048]{1,0:T(8,128)}) %all-gather.9.cloned.1.call-update) | async-done | bytes 3670032 | tf_op jit(solution)/shard_map/all_gather | solution.py:51
  106.5 4.1 convolution_multiply_fusion.3
  110.8 2.0 gather_fusion.1
  112.8 136.9 %reduce-scatter.7.cloned.1.call-done = f32[8,2048]{1,0:T(8,128)} async-done(((f32[256,2048]{1,0:T(8,128)}), f32[8,2048]{1,0:T(8,128)}) %reduce-scatter.7.cloned.1.call-update) | async-done | bytes 65552 | tf_op jit(solution)/shard_map/reduce_scatter | solution.py:71
  249.7 1.5 multiply_convert_fusion.15
  251.8 1.4 gather_fusion.2
  253.2 147.6 %all-gather.11.cloned.1.call-done = bf16[256,2048]{1,0:T(8,128)(2,1)} async-done(((bf16[8,2048]{1,0:T(8,128)(2,1)}), bf16[256,2048]{1,0:T(8,128)(2,1)}) %all-gather.11.cloned.1.call-update) | async-done | bytes 1048592 | tf_op jit(solution)/shard_map/all_gather | solution.py:82
  400.8 3.5 fusion.59
  404.6 12.1 fusion.73
  418.2 1.5 multiply_convert_fusion.8
  421.3 4.4 multiply_subtract_fusion.5
  425.6 1.8 copy-done.3
  427.4 2.1 convolution_multiply_fusion.2
  429.7 2.0 gather_fusion.3
  431.7 158.7 %reduce-scatter.9.cloned.1.call-done = f32[8,2048]{1,0:T(8,128)} async-done(((f32[256,2048]{1,0:T(8,128)}), f32[8,2048]{1,0:T(8,128)}) %reduce-scatter.9.cloned.1.call-update) | async-done | bytes 65552 | tf_op jit(solution)/shard_map/reduce_scatter | solution.py:71
  590.4 1.5 multiply_convert_fusion.14
  592.2 1.4 gather_fusion.4
  593.6 148.6 %all-gather.13.cloned.1.call-done = bf16[256,2048]{1,0:T(8,128)(2,1)} async-done(((bf16[8,2048]{1,0:T(8,128)(2,1)}), bf16[256,2048]{1,0:T(8,128)(2,1)}) %all-gather.13.cloned.1.call-update) | async-done | bytes 1048592 | tf_op jit(solution)/shard_map/all_gather | solution.py:82
  742.2 3.5 fusion.60
  745.9 16.8 %fusion.71 = (bf16[2,2048,448]{1,2,0:T(8,128)(2,1)S(1)}, f32[2,2048,448]{1,2,0:T(8,128)}, f32[2,2048,448]{1,2,0:T(8,128)}) fusion(f32[2,2048,448]{1,2,0:T(8,128)} %get-tuple-element.25, f32[2,448,2048]{2,1,0:T(8,128)} %get-tuple-element.46, bf16[1,2,2048,448]{2,3,1,0:T(8,128)(2,1)S(1)} %copy-done.23, bf16[1,2,2048,448]{2,3,1,0:T(8,128)(2,1)} %param.24, ...), kind=kOutput, calls=%fused_computation.174 | convolution fusion | flops 986152960 | bytes 41877760 | tf_op jit(solution)/shard_map/td,ktf->kdf/dot_general | solution.py:101
  763.5 1.5 multiply_convert_fusion.5
  767.7 5.9 multiply_subtract_fusion.4
  773.6 1.8 copy-done.5
  775.4 2.0 convolution_multiply_fusion.1
  777.6 2.0 gather_fusion.5
  779.6 158.6 %reduce-scatter.11.cloned.1.call-done = f32[8,2048]{1,0:T(8,128)} async-done(((f32[256,2048]{1,0:T(8,128)}), f32[8,2048]{1,0:T(8,128)}) %reduce-scatter.11.cloned.1.call-update) | async-done | bytes 65552 | tf_op jit(solution)/shard_map/reduce_scatter | solution.py:71
  938.2 1.5 multiply_convert_fusion.13
  941.5 149.3 %all-gather.15.cloned.1.call-done = bf16[256,2048]{1,0:T(8,128)(2,1)} async-done(((bf16[8,2048]{1,0:T(8,128)(2,1)}), bf16[256,2048]{1,0:T(8,128)(2,1)}) %all-gather.15.cloned.1.call-update) | async-done | bytes 1048592 | tf_op jit(solution)/shard_map/all_gather | solution.py:82
  1090.7 3.3 fusion.61
  1094.0 16.6 %fusion.72 = (bf16[2,2048,448]{1,2,0:T(8,128)(2,1)S(1)}, f32[2,2048,448]{1,2,0:T(8,128)}, f32[2,448,2048]{2,1,0:T(8,128)}) fusion(f32[2,2048,448]{1,2,0:T(8,128)} %get-tuple-element.20, f32[2,2048,448]{1,2,0:T(8,128)} %get-tuple-element.21, f32[2,2048,448]{1,2,0:T(8,128)} %get-tuple-element.25, bf16[256,2048]{1,0:T(8,128)(2,1)S(1)} %gather_fusion.4, ...), kind=kOutput, calls=%fused_computation.175 | convolution fusion | flops 978812928 | bytes 41877760 | tf_op jit(solution)/shard_map/td,ktf->kdf/dot_general | solution.py:101
  1115.3 4.3 multiply_subtract_fusion.3
  1119.6 1.8 copy-done.7
  1121.5 2.0 convolution_multiply_fusion
  1123.6 2.0 gather_fusion.7
  1125.6 158.8 %reduce-scatter.13.cloned.1.call-done = f32[8,2048]{1,0:T(8,128)} async-done(((f32[256,2048]{1,0:T(8,128)}), f32[8,2048]{1,0:T(8,128)}) %reduce-scatter.13.cloned.1.call-update) | async-done | bytes 65552 | tf_op jit(solution)/shard_map/reduce_scatter | solution.py:71
  1284.5 1.5 multiply_convert_fusion.12
  1286.3 150.2 %all-gather.17.cloned.1.call-done = bf16[256,2048]{1,0:T(8,128)(2,1)} async-done(((bf16[8,2048]{1,0:T(8,128)(2,1)}), bf16[256,2048]{1,0:T(8,128)(2,1)}) %all-gather.17.cloned.1.call-update) | async-done | bytes 1048592 | tf_op jit(solution)/shard_map/all_gather | solution.py:82
  1436.5 11.9 subtract_convert_fusion
  1448.5 2.8 fusion.62
  1451.3 17.1 %fusion.7 = bf16[2,2048,448]{1,2,0:T(8,128)(2,1)} fusion(f32[2,2048,448]{1,2,0:T(8,128)} %all-gather.7.cloned.1.call-done, f32[2,2048,448]{1,2,0:T(8,128)} %get-tuple-element.13, f32[2,448,2048]{2,1,0:T(8,128)} %get-tuple-element.53, f32[2,2048,448]{1,2,0:T(8,128)} %get-tuple-element.21, f32[2,2048,448]{1,2,0:T(8,128)} %get-tuple-element.20, ...), kind=kOutput, calls=%fused_computation.26 | convolution fusion | flops 984317952 | bytes 41877760 | tf_op jit(solution)/shard_map/td,ktf->kdf/dot_general | solution.py:101
  1468.4 38.8 %reduce-scatter.17.cloned.1.call-done = bf16[448,512]{1,0:T(8,128)(2,1)} async-done(((bf16[448,2048]{1,0:T(8,128)(2,1)}), bf16[448,512]{1,0:T(8,128)(2,1)}) %reduce-scatter.17.cloned.1.call-update) | async-done | bytes 458768 | tf_op jit(solution)/shard_map/reduce_scatter | solution.py:114
  1507.2 3.2 multiply_subtract_fusion.7
  1510.5 47.0 %reduce-scatter.15.cloned.1.call-done = bf16[2,512,448]{1,2,0:T(8,128)(2,1)} async-done(((bf16[2,2048,448]{1,2,0:T(8,128)(2,1)}), bf16[2,512,448]{1,2,0:T(8,128)(2,1)}) %reduce-scatter.15.cloned.1.call-update) | async-done | bytes 917520 | tf_op jit(solution)/shard_map/reduce_scatter | solution.py:111
  1557.5 4.3 multiply_subtract_fusion.6
  (109 shorter events, 19.1 us)
Async XLA Ops:
  7.2 2.4 copy-start
  7.2 62.7 %all-gather.7.cloned.1.call-start = ((), (), s32[]{:S(2)}) async-start(), calls=%async_computation.6 | async-start | bytes 9175040 | tf_op jit(solution)/shard_map/all_gather | solution.py:50
  7.9 98.5 %all-gather.9.cloned.1.call-start = ((), (), s32[]{:S(2)}) async-start(), calls=%async_computation.7 | async-start | bytes 4587520 | tf_op jit(solution)/shard_map/all_gather | solution.py:51
  8.7 241.0 %reduce-scatter.7.cloned.1.call-start = ((), (), s32[]{:S(2)}) async-start(), calls=%async_computation.8 | async-start | bytes 2162688 | tf_op jit(solution)/shard_map/reduce_scatter | solution.py:71
  74.3 0.8 copy-start.15
  106.5 4.2 copy-start.21
  110.6 290.2 %all-gather.11.cloned.1.call-start = ((), (), s32[]{:S(2)}) async-start(), calls=%async_computation.9 | async-start | bytes 1081344 | tf_op jit(solution)/shard_map/all_gather | solution.py:82
  251.2 339.2 %reduce-scatter.9.cloned.1.call-start = ((), (), s32[]{:S(2)}) async-start(), calls=%async_computation.10 | async-start | bytes 2162688 | tf_op jit(solution)/shard_map/reduce_scatter | solution.py:71
  253.2 164.2 %copy-start.9 = (bf16[256,2048]{1,0:T(8,128)(2,1)}, bf16[256,2048]{1,0:T(8,128)(2,1)S(1)}, u32[]{:S(2)}) copy-start(bf16[256,2048]{1,0:T(8,128)(2,1)S(1)} %gather_fusion.2) | copy-start | bytes 3145732
  400.8 3.7 copy-start.22
  416.6 3.1 copy-start.26
  417.4 0.8 copy-start.17
  418.2 2.2 copy-start.2
  418.2 2.5 copy-start.13
  418.2 3.1 copy-start.24
  421.3 4.4 copy-start.18
  425.6 1.8 copy-start.3
  429.6 312.6 %all-gather.13.cloned.1.call-start = ((), (), s32[]{:S(2)}) async-start(), calls=%async_computation.11 | async-start | bytes 1081344 | tf_op jit(solution)/shard_map/all_gather | solution.py:82
  591.9 346.3 %reduce-scatter.11.cloned.1.call-start = ((), (), s32[]{:S(2)}) async-start(), calls=%async_computation.12 | async-start | bytes 2162688 | tf_op jit(solution)/shard_map/reduce_scatter | solution.py:71
  593.5 152.1 %copy-start.10 = (bf16[256,2048]{1,0:T(8,128)(2,1)S(1)}, bf16[256,2048]{1,0:T(8,128)(2,1)}, u32[]{:S(2)}) copy-start(bf16[256,2048]{1,0:T(8,128)(2,1)} %copy-done.9) | copy-start | bytes 3145732
  742.2 3.7 copy-start.23
  762.7 2.4 copy-start.27
  762.7 2.9 copy-start.30
  763.5 1.6 copy-start.16
  763.5 3.4 copy-start.4
  763.5 3.6 copy-start.11
  763.5 3.6 copy-start.19
  763.5 4.2 copy-start.25
  773.6 1.8 copy-start.5
  777.5 313.2 %all-gather.15.cloned.1.call-start = ((), (), s32[]{:S(2)}) async-start(), calls=%async_computation.13 | async-start | bytes 1081344 | tf_op jit(solution)/shard_map/all_gather | solution.py:82
  939.8 344.7 %reduce-scatter.13.cloned.1.call-start = ((), (), s32[]{:S(2)}) async-start(), calls=%async_computation.14 | async-start | bytes 2162688 | tf_op jit(solution)/shard_map/reduce_scatter | solution.py:71
  1110.6 2.0 copy-start.28
  1110.6 3.2 copy-start.29
  1111.4 3.7 copy-start.6
  1111.4 3.9 copy-start.12
  1112.2 7.4 copy-start.20
  1119.6 1.9 copy-start.7
  1123.5 313.0 %all-gather.17.cloned.1.call-start = ((), (), s32[]{:S(2)}) async-start(), calls=%async_computation.15 | async-start | bytes 1081344 | tf_op jit(solution)/shard_map/all_gather | solution.py:82
  1286.0 221.2 %reduce-scatter.17.cloned.1.call-start = ((), (), s32[]{:S(2)}) async-start(), calls=%async_computation.17 | async-start | bytes 2293760 | tf_op jit(solution)/shard_map/reduce_scatter | solution.py:114
  1436.5 12.0 copy-start.14
  1448.5 109.0 %reduce-scatter.15.cloned.1.call-start = ((), (), s32[]{:S(2)}) async-start(), calls=%async_computation.16 | async-start | bytes 4587520 | tf_op jit(solution)/shard_map/reduce_scatter | solution.py:111
  1468.4 89.1 %copy-start.8 = (f32[2,512,448]{1,2,0:T(8,128)S(1)}, f32[2,512,448]{1,2,0:T(8,128)}, u32[]{:S(2)}) copy-start(f32[2,512,448]{1,2,0:T(8,128)} %param.20) | copy-start | bytes 5505028
  1507.2 54.5 %copy-start.1 = (bf16[1,256,2048]{2,1,0:T(8,128)(2,1)S(1)}, bf16[1,256,2048]{2,1,0:T(8,128)(2,1)}, u32[]{:S(2)}) copy-start(bf16[1,256,2048]{2,1,0:T(8,128)(2,1)} %param.16) | copy-start | bytes 3145732
Sparse Core Ops, SparseCore 0:
  9.7 60.1 all-gather.6
  71.5 34.8 all-gather.8
  110.8 138.8 reduce-scatter.6
  251.8 148.9 all-gather.10
  429.7 160.6 reduce-scatter.8
  592.0 150.1 all-gather.12
  777.6 160.5 reduce-scatter.10
  940.6 150.1 all-gather.14
  1123.6 160.7 reduce-scatter.12
  1286.5 149.9 all-gather.16
  1448.6 58.6 reduce-scatter.16
  1509.9 47.5 reduce-scatter.14
where the time goes:
time: 1570 us
  waiting for transfers between devices  1380 us (88%)
  matrix products  121 us (8%)
  local copies, waits for them, and re-layouts  29.1 us (2%)
  other arithmetic  17.7 us (1%)
    reduce_scatter x4, waiting for transfers between devices, on_device(): lax.psum_scatter(jnp.dot(hidden, down_b, preferred_element_type=jnp.float...  613 us
    all_gather x4, waiting for transfers between devices, on_device(): out_grad = lax.all_gather(own_grad, 'fsdp', axis=0, tiled=True)  596 us
    dot_general x4, matrix products, on_device(): jnp.einsum('td,ktf->kdf', inputs, pre_grad, preferred_element_type=jnp.fl...  62.6 us
    all_gather x1, waiting for transfers between devices, on_device(): lax.all_gather(gate_up, 'rep', axis=1, tiled=True)  58.9 us
    reduce_scatter x1, waiting for transfers between devices, on_device(): lax.psum_scatter(delta_gu.astype(jnp.bfloat16), 'rep', scatter_dimension=...  47 us
    reduce_scatter x1, waiting for transfers between devices, on_device(): lax.psum_scatter(delta_down.astype(jnp.bfloat16), 'rep', scatter_dimensio...  38.8 us
  transfers between devices with their start and end apart: 12, of which 12 were waited for; matrix products, arithmetic and copies ran while one was open for 3% of the time, Pallas kernels for 0%

commit v1 on v0

v1 whole, which is shorter than its diff:
```python
import functools
import math

import jax
import jax.numpy as jnp
from jax import lax
from jax.experimental import pallas as pl
from jax.experimental.pallas import tpu as pltpu
from jax.sharding import PartitionSpec as P

D = 2048
FF = 14336
STEPS = 4
TOK = 256
ROWS = 256
SHARDS = 32
HID = FF // SHARDS
SIDE = 4
BLOCKS = 4
BW = D // BLOCKS
BAND = TOK // SIDE
OWN = BAND // SIDE
HALF = BW // 2

beta_one = 0.9
beta_two = 0.95
inner_rate = 0.03
decay_rate = 0.1
epsilon = 1e-08
outer_rate = 0.7
momentum_rate = 0.9

in_scale = 1.0 / D**0.5
out_scale = 1.0 / FF**0.5
first_gain = inner_rate
step_gain = first_gain * (1.0 - beta_one)
second_gain = step_gain**2 / (1.0 - beta_two)
root_gain = math.sqrt(second_gain)
keep_rate = 1.0 - inner_rate * decay_rate

MESH = pl.DeviceIdType.MESH
VMEM = pltpu.VMEM
F32 = jnp.float32
BF16 = jnp.bfloat16


def adam(weight, grad, first, second, gain):
    t = grad * gain
    first = beta_one * first + t
    second = beta_two * second + t * t
    root = second * lax.rsqrt(second) + epsilon * root_gain
    move = first * pl.reciprocal(root, approx=True)
    return keep_rate * weight - root_gain * move, first, second


def inner_kernel(
    in_row_ids,
    in_col_ids,
    target_col_ids,
    table,
    table_t,
    targets,
    gu_hbm,
    down_hbm,
    m_gu_hbm,
    v_gu_hbm,
    m_down_hbm,
    v_down_hbm,
    p_gu_hbm,
    p_down_hbm,
    w_gu,
    m_gu,
    v_gu,
    b_gu,
    w_down,
    m_down,
    v_down,
    b_down,
    s_down,
    stage_gu,
    stage_down,
    inputs,
    inputs_t,
    pick,
    wanted,
    gate_buf,
    up_buf,
    slope_buf,
    silu_buf,
    hidden,
    hidden_t,
    hidden_grad,
    pre_grad,
    grad,
    partial,
    land_one,
    sum_one,
    land_two,
    out_grad,
    load_sem,
    gu_sem,
    down_sem,
    send_sem,
    recv_sem,
):
    rep = lax.axis_index("rep")
    fsdp = lax.axis_index("fsdp")
    zl = fsdp // (SIDE * SIDE)
    side = ((fsdp // SIDE) % SIDE, fsdp % SIDE)

    def peer(part, d_first, d_second, d_z):
        first = (side[part] + d_first) % SIDE
        second = (side[1 - part] + d_second) % SIDE
        z = (zl + d_z) % 2
        x, y = (first, second) if part == 0 else (second, first)
        return (rep, z * SIDE * SIDE + x * SIDE + y)

    cross = [(ds, dz) for ds in range(SIDE) for dz in range(2) if (ds, dz) != (0, 0)]
    partners = [peer(0, o, 0, dz) for o in range(1, SIDE) for dz in range(2)]
    partners += [peer(0, 0, ds, dz) for ds, dz in cross]

    barrier = pltpu.get_barrier_semaphore()
    for other in partners:
        pl.semaphore_signal(barrier, inc=1, device_id=other, device_id_type=MESH)

    load_gu = pltpu.make_async_copy(gu_hbm, b_gu, load_sem.at[0])
    load_down = pltpu.make_async_copy(down_hbm, b_down, load_sem.at[1])
    load_start = pltpu.make_async_copy(down_hbm, s_down, load_sem.at[2])
    load_gu.start()
    load_down.start()
    load_start.start()

    pieces = D // ROWS

    def gu_piece(i, slot):
        rows = pl.ds(pl.multiple_of((i % pieces) * ROWS, ROWS), ROWS)
        return [
            pltpu.make_async_copy(
                source.at[i // pieces, rows, :], stage_gu.at[slot, n], gu_sem.at[slot, n]
            )
            for n, source in enumerate((m_gu_hbm, v_gu_hbm))
        ]

    def down_piece(q, slot):
        return [
            pltpu.make_async_copy(
                source.at[:, pl.ds(q * BW, BW)], stage_down.at[slot, n], down_sem.at[slot, n]
            )
            for n, source in enumerate((m_down_hbm, v_down_hbm))
        ]

    for slot in range(2):
        for copy in gu_piece(slot, slot) + down_piece(slot, slot):
            copy.start()

    def load_gu_moments(i, carry):
        slot = i % 2
        for copy in gu_piece(i, slot):
            copy.wait()
        for r in range(0, ROWS, 64):
            rows = pl.ds(pl.multiple_of((i % pieces) * ROWS + r, 64), 64)
            m_gu[i // pieces, rows, :] = stage_gu[slot, 0, r : r + 64, :].astype(F32) * first_gain
            v_gu[i // pieces, rows, :] = stage_gu[slot, 1, r : r + 64, :].astype(F32) * second_gain

        @pl.when(i + 2 < 2 * pieces)
        def _():
            for copy in gu_piece(i + 2, slot):
                copy.start()

        return carry

    lax.fori_loop(0, 2 * pieces, load_gu_moments, 0)
    for q in range(BLOCKS):
        slot = q % 2
        for copy in down_piece(q, slot):
            copy.wait()
        cols = pl.ds(q * BW, BW)

        def load_down_moments(i, carry):
            rows = pl.ds(pl.multiple_of(i * 64, 64), 64)
            m_down[rows, cols] = stage_down[slot, 0, rows, :].astype(F32) * first_gain
            v_down[rows, cols] = stage_down[slot, 1, rows, :].astype(F32) * second_gain
            return carry

        lax.fori_loop(0, HID // 64, load_down_moments, 0)
        if q + 2 < BLOCKS:
            for copy in down_piece(q + 2, slot):
                copy.start()

    load_gu.wait()
    load_down.wait()
    load_start.wait()

    def widen_gu(i, carry):
        rows = pl.ds(pl.multiple_of((i % 32) * 64, 64), 64)
        w_gu[i // 32, rows, :] = b_gu[i // 32, rows, :].astype(F32)
        return carry

    lax.fori_loop(0, 64, widen_gu, 0)

    def widen_down(i, carry):
        rows = pl.ds(pl.multiple_of(i * 16, 16), 16)
        w_down[rows, :] = b_down[rows, :].astype(F32)
        return carry

    lax.fori_loop(0, HID // 16, widen_down, 0)

    def look_up_inputs(k):
        rows = lax.broadcasted_iota(jnp.int32, (TOK, ROWS), 1)
        chosen = (in_col_ids[k] == rows).astype(F32).astype(BF16)
        inputs[...] = jnp.dot(chosen, table[...], preferred_element_type=F32).astype(BF16)

    look_up_inputs(0)
    pl.semaphore_wait(barrier, len(partners))

    def band(coordinate):
        return pl.ds(pl.multiple_of(coordinate * BAND, BAND), BAND)

    def own_rows(first, second):
        return pl.ds(pl.multiple_of(first * BAND + second * OWN, OWN), OWN)

    def own_cols(z):
        return pl.ds(pl.multiple_of(z * HALF, HALF), HALF)

    def send(kind, q, src, dst, other):
        pltpu.make_async_remote_copy(
            src_ref=src,
            dst_ref=dst,
            send_sem=send_sem.at[kind, q],
            recv_sem=recv_sem.at[kind, q],
            device_id=other,
            device_id_type=MESH,
        ).start()

    def wait_bytes(kind, q, sem):
        like = land_one.at[q] if kind in (0, 3) else land_two.at[q]
        pltpu.make_async_copy(like, like, sem.at[kind, q]).wait()

    def scatter_one(q):
        part = q % 2
        for o in range(1, SIDE):
            to = (side[part] + o) % SIDE
            send(0, q, partial.at[q, band(to), :], land_one.at[q, o - 1], peer(part, o, 0, 0))

    def scatter_two(q):
        part = q % 2
        wait_bytes(0, q, recv_sem)
        total = partial[q, band(side[part]), :].astype(F32)
        for o in range(SIDE - 1):
            total = total + land_one[q, o].astype(F32)
        sum_one[q] = total.astype(BF16)
        for n, (ds, dz) in enumerate(cross):
            to = (side[1 - part] + ds) % SIDE
            rows = pl.ds(pl.multiple_of(to * OWN, OWN), OWN)
            src = sum_one.at[q, rows, own_cols((zl + dz) % 2)]
            send(1, q, src, land_two.at[q, n], peer(part, 0, ds, dz))

    def gather_one(q):
        part = q % 2
        wait_bytes(1, q, recv_sem)
        rows = pl.ds(pl.multiple_of(side[1 - part] * OWN, OWN), OWN)
        total = sum_one[q, rows, own_cols(zl)].astype(F32)
        for n in range(len(cross)):
            total = total + land_two[q, n].astype(F32)
        mine = (q, own_rows(side[part], side[1 - part]), own_cols(zl))
        out_grad[mine] = ((total - wanted[q]) * (1.0 / TOK)).astype(BF16)
        for ds, dz in cross:
            send(2, q, out_grad.at[mine], out_grad.at[mine], peer(part, 0, ds, dz))

    def gather_two(q):
        part = q % 2
        wait_bytes(2, q, recv_sem)
        mine = out_grad.at[q, band(side[part]), :]
        for o in range(1, SIDE):
            send(3, q, mine, mine, peer(part, o, 0, 0))

    def update_down(q, last):
        cols = pl.ds(q * BW, BW)

        def rows_of(i, carry):
            rows = pl.ds(pl.multiple_of(i * 16, 16), 16)
            weight, first, second = adam(
                w_down[rows, cols],
                grad[rows, :],
                m_down[rows, cols],
                v_down[rows, cols],
                step_gain * out_scale,
            )
            if last:
                b_down[rows, cols] = (s_down[rows, cols].astype(F32) - weight).astype(BF16)
            else:
                w_down[rows, cols] = weight
                m_down[rows, cols] = first
                v_down[rows, cols] = second
                b_down[rows, cols] = weight.astype(BF16)
            return carry

        lax.fori_loop(0, HID // 16, rows_of, 0, unroll=2)

    def update_gu(j, base, last):
        def rows_of(i, carry):
            here = pl.ds(pl.multiple_of(i * 16, 16), 16)
            rows = pl.ds(pl.multiple_of(base + i * 16, 16), 16)
            weight, first, second = adam(
                w_gu[j, rows, :],
                grad[here, :HID],
                m_gu[j, rows, :],
                v_gu[j, rows, :],
                step_gain * in_scale,
            )
            if last:
                b_gu[j, rows, :] = (b_gu[j, rows, :].astype(F32) - weight).astype(BF16)
            else:
                w_gu[j, rows, :] = weight
                m_gu[j, rows, :] = first
                v_gu[j, rows, :] = second
                b_gu[j, rows, :] = weight.astype(BF16)
            return carry

        lax.fori_loop(0, ROWS // 16, rows_of, 0, unroll=2)

    def use_block(q, k):
        wait_bytes(3, q, recv_sem)
        cols = pl.ds(q * BW, BW)
        product = lax.dot_general(
            out_grad[q], b_down[:, cols], (((1,), (1,)), ((), ())), preferred_element_type=F32
        )
        if q == 0:
            hidden_grad[...] = product
        else:
            hidden_grad[...] += product
        grad[:HID, :] = jnp.dot(hidden_t[...], out_grad[q], preferred_element_type=F32)

        @pl.when(k < STEPS - 1)
        def _():
            update_down(q, False)

        @pl.when(k == STEPS - 1)
        def _():
            update_down(q, True)

    def step(k, carry):
        gate_buf[...] = jnp.dot(inputs[...], b_gu[0], preferred_element_type=F32)
        up_buf[...] = jnp.dot(inputs[...], b_gu[1], preferred_element_type=F32)

        @pl.when(k == STEPS - 1)
        def _():
            load_gu.start()

        def activate(i, carry):
            rows = pl.ds(pl.multiple_of(i * 32, 32), 32)
            gate = gate_buf[rows, :] * in_scale
            upper = up_buf[rows, :] * in_scale
            sigmoid = jax.nn.sigmoid(gate)
            silu = gate * sigmoid
            hidden[rows, :] = (silu * upper).astype(BF16)
            silu_buf[rows, :] = silu * out_scale
            slope_buf[rows, :] = upper * sigmoid * (1.0 + gate * (1.0 - sigmoid)) * out_scale
            return carry

        lax.fori_loop(0, TOK // 32, activate, 0)

        for q in range(BLOCKS):
            cols = pl.ds(q * BW, BW)
            product = jnp.dot(hidden[...], b_down[:, cols], preferred_element_type=F32)
            partial[q] = (product * out_scale).astype(BF16)
            scatter_one(q)

        hidden_t[...] = hidden[...].T
        rows = lax.broadcasted_iota(jnp.int32, (TOK, ROWS), 1)
        pick[...] = (target_col_ids[k] == rows).astype(F32).astype(BF16)
        for q in range(BLOCKS):
            part = q % 2
            chosen = pick[own_rows(side[part], side[1 - part]), :]
            cols = pl.ds(pl.multiple_of(q * BW + zl * HALF, HALF), HALF)
            wanted[q] = jnp.dot(chosen, targets[:, cols], preferred_element_type=F32)
        tall = lax.broadcasted_iota(jnp.int32, (ROWS, TOK), 0)
        chosen_t = (in_row_ids[k] == tall).astype(F32).astype(BF16)
        inputs_t[...] = jnp.dot(table_t[...], chosen_t, preferred_element_type=F32).astype(BF16)
        look_up_inputs(jnp.minimum(k + 1, STEPS - 1))

        scatter_two(0)
        scatter_two(1)
        gather_one(0)
        scatter_two(2)
        gather_one(1)
        scatter_two(3)
        gather_two(0)
        gather_one(2)
        gather_two(1)
        gather_one(3)
        gather_two(2)
        use_block(0, k)
        gather_two(3)
        use_block(1, k)
        use_block(2, k)
        use_block(3, k)

        pre_grad[0] = (hidden_grad[...] * slope_buf[...]).astype(BF16)
        pre_grad[1] = (hidden_grad[...] * silu_buf[...]).astype(BF16)

        @pl.when(k == STEPS - 1)
        def _():
            load_gu.wait()

        def update_piece(i, carry):
            base = pl.multiple_of(i * ROWS, ROWS)
            for j in range(2):
                grad[:ROWS, :HID] = jnp.dot(
                    inputs_t[pl.ds(base, ROWS), :], pre_grad[j], preferred_element_type=F32
                )

                @pl.when(k < STEPS - 1)
                def _():
                    update_gu(j, base, False)

                @pl.when(k == STEPS - 1)
                def _():
                    update_gu(j, base, True)

            return carry

        lax.fori_loop(0, D // ROWS, update_piece, 0)

        for q in range(BLOCKS):
            for kind in range(4):
                wait_bytes(kind, q, send_sem)
        return carry

    lax.fori_loop(0, STEPS, step, 0)

    store_gu = pltpu.make_async_copy(b_gu, p_gu_hbm, load_sem.at[0])
    store_down = pltpu.make_async_copy(b_down, p_down_hbm, load_sem.at[1])
    store_gu.start()
    store_down.start()
    store_gu.wait()
    store_down.wait()


def inner_steps(in_ids, target_ids, table, targets, gu, down, m_gu, v_gu, m_down, v_down):
    in_vmem = pl.BlockSpec(memory_space=VMEM)
    anywhere = pl.BlockSpec(memory_space=pl.ANY)
    gu_shape, down_shape = (2, D, HID), (HID, D)
    return pl.pallas_call(
        inner_kernel,
        out_shape=(
            jax.ShapeDtypeStruct(gu_shape, BF16),
            jax.ShapeDtypeStruct(down_shape, BF16),
        ),
        in_specs=[in_vmem] * 6 + [anywhere] * 6,
        out_specs=(anywhere, anywhere),
        scratch_shapes=[
            VMEM(gu_shape, F32),
            VMEM(gu_shape, F32),
            VMEM(gu_shape, F32),
            VMEM(gu_shape, BF16),
            VMEM(down_shape, F32),
            VMEM(down_shape, F32),
            VMEM(down_shape, F32),
            VMEM(down_shape, BF16),
            VMEM(down_shape, BF16),
            VMEM((2, 2, ROWS, HID), BF16),
            VMEM((2, 2, HID, BW), BF16),
            VMEM((TOK, D), BF16),
            VMEM((D, TOK), BF16),
            VMEM((TOK, ROWS), BF16),
            VMEM((BLOCKS, OWN, HALF), F32),
            VMEM((TOK, HID), F32),
            VMEM((TOK, HID), F32),
            VMEM((TOK, HID), F32),
            VMEM((TOK, HID), F32),
            VMEM((TOK, HID), BF16),
            VMEM((HID, TOK), BF16),
            VMEM((TOK, HID), F32),
            VMEM((2, TOK, HID), BF16),
            VMEM((HID, BW), F32),
            VMEM((BLOCKS, TOK, BW), BF16),
            VMEM((BLOCKS, SIDE - 1, BAND, BW), BF16),
            VMEM((BLOCKS, BAND, BW), BF16),
            VMEM((BLOCKS, 2 * SIDE - 1, OWN, HALF), BF16),
            VMEM((BLOCKS, TOK, BW), BF16),
            pltpu.SemaphoreType.DMA((3,)),
            pltpu.SemaphoreType.DMA((2, 2)),
            pltpu.SemaphoreType.DMA((2, 2)),
            pltpu.SemaphoreType.DMA((4, BLOCKS)),
            pltpu.SemaphoreType.DMA((4, BLOCKS)),
        ],
        compiler_params=pltpu.CompilerParams(
            collective_id=0, has_side_effects=True, vmem_limit_bytes=60 * 2**20
        ),
        name="inner_steps",
    )(
        in_ids[:, None, :],
        in_ids[:, :, None],
        target_ids[:, :, None],
        table,
        table.T,
        targets,
        gu,
        down,
        m_gu,
        v_gu,
        m_down,
        v_down,
    )


def on_device(
    in_table,
    target_table,
    in_ids,
    target_ids,
    gate_up,
    down,
    mom_gate_up,
    mom_down,
    m_gate_up,
    v_gate_up,
    m_down,
    v_down,
):
    start_gu = lax.all_gather(gate_up.astype(BF16), "rep", axis=1, tiled=True)
    start_down = lax.all_gather(down.astype(BF16), "rep", axis=1, tiled=True)
    delta_gu, delta_down = inner_steps(
        in_ids[0],
        target_ids[0],
        in_table[0],
        target_table[0],
        start_gu,
        start_down,
        m_gate_up[0],
        v_gate_up[0],
        m_down[0],
        v_down[0],
    )
    total_gu = lax.psum_scatter(delta_gu, "rep", scatter_dimension=1, tiled=True).astype(F32)
    total_down = lax.psum_scatter(delta_down, "rep", scatter_dimension=1, tiled=True).astype(F32)
    replicas = lax.axis_size("rep")
    mean_gu = total_gu / replicas
    mean_down = total_down / replicas
    new_mom_gu = momentum_rate * mom_gate_up + mean_gu
    new_mom_down = momentum_rate * mom_down + mean_down
    new_gu = gate_up - outer_rate * (mean_gu + momentum_rate * new_mom_gu)
    new_down = down - outer_rate * (mean_down + momentum_rate * new_mom_down)
    return (new_gu, new_down, new_mom_gu, new_mom_down)


def solution(mesh):
    in_specs = (
        P("rep", None, None),
        P("rep", None, None),
        P("rep", None, None),
        P("rep", None, None),
        P(None, "rep", "fsdp"),
        P("fsdp", "rep"),
        P(None, "rep", "fsdp"),
        P("fsdp", "rep"),
        P("rep", None, None, "fsdp"),
        P("rep", None, None, "fsdp"),
        P("rep", "fsdp", None),
        P("rep", "fsdp", None),
    )
    out_specs = (P(None, "rep", "fsdp"), P("fsdp", "rep"), P(None, "rep", "fsdp"), P("fsdp", "rep"))
    return jax.shard_map(
        on_device, mesh=mesh, in_specs=in_specs, out_specs=out_specs, check_vma=False
    )
```

time: 1570 us -> 355 us (0.23)
  waiting for transfers between devices: 1380 us -> 147 us
  Pallas kernels: 0 us -> 156 us
  matrix products: 121 us -> 0 us
    all_gather x6 -> x2, waiting for transfers between devices: 685 us -> 51.4 us  [the longest x1 40.2 us: on_device(): start_gu = lax.all_gather(gate_up.astype(BF16), 'rep', axis=1, tiled=True)]
    reduce_scatter x6 -> x2, waiting for transfers between devices: 699 us -> 94.8 us  [the longest x1 50.6 us: on_device(): lax.psum_scatter(delta_gu, 'rep', scatter_dimension=1, tiled=True)]
    pallas_call x0 -> x1, Pallas kernels: none -> 156 us  [inner_steps(): pl.pallas_call(inner_kernel, out_shape=(jax.ShapeDtypeStruct(gu_shape, BF...]
    dot_general x24 -> x0, matrix products: 121 us -> none  [the longest x4 62.6 us: on_device(): jnp.einsum('td,ktf->kdf', inputs, pre_grad, preferred_element_type=jnp.fl...]
  transfers between devices with their start and end apart: 12 -> 4, of which waited for: 12 -> 4; matrix products, arithmetic and copies ran while one was open for 3% -> 7% of each run, Pallas kernels for 0% -> 0%
where the time goes in v1:
time: 355 us; the launch traced here: 354 us
  Pallas kernels  156 us (44%)
  waiting for transfers between devices  147 us (41%)
  local copies, waits for them, and re-layouts  27.3 us (8%)
  between operations  13.8 us (4%)
  other arithmetic  9.74 us (3%)
    pallas_call x1, Pallas kernels, inner_steps(): pl.pallas_call(inner_kernel, out_shape=(jax.ShapeDtypeStruct(gu_shape, BF...  156 us
    reduce_scatter x1, waiting for transfers between devices, on_device(): lax.psum_scatter(delta_gu, 'rep', scatter_dimension=1, tiled=True)  50.6 us
    reduce_scatter x1, waiting for transfers between devices, on_device(): lax.psum_scatter(delta_down, 'rep', scatter_dimension=1, tiled=True)  44.2 us
    all_gather x1, waiting for transfers between devices, on_device(): start_gu = lax.all_gather(gate_up.astype(BF16), 'rep', axis=1, tiled=True)  40.2 us
    unnamed x19, local copies, waits for them, and re-layouts  23.4 us
    all_gather x1, waiting for transfers between devices, on_device(): start_down = lax.all_gather(down.astype(BF16), 'rep', axis=1, tiled=True)  11.2 us
  transfers between devices with their start and end apart: 4, of which 4 were waited for; matrix products, arithmetic and copies ran while one was open for 7% of the time, Pallas kernels for 0%

profile of v1, /device:TPU:1, one launch (start us, length us, event | category | flops | bytes accessed | tf_op | source)
XLA Modules:
  0.0 353.9 jit_solution(4370040107858565098)
XLA Ops:
  7.2 0.0 copy-start.1
  7.2 0.0 all-gather.5.cloned.1.call-start
  7.2 2.1 convert_element_type.13
  9.4 0.0 all-gather.5.cloned.1.call-update
  9.4 0.0 all-gather.3.cloned.1.call-start
  9.4 0.0 copy-done.1
  9.4 0.1 convert_element_type.12
  9.6 1.3 copy.37
  10.9 0.0 all-gather.3.cloned.1.call-update
  10.9 0.0 reduce-scatter.5.cloned.1.call-start
  10.9 6.2 %copy.38 = bf16[1,2,2048,448]{3,2,1,0:T(8,128)(2,1)} copy(bf16[1,2,2048,448]{2,3,1,0:T(8,128)(2,1)} %param.20) | data formatting | bytes 7340032 | tf_op args[8]
  17.2 0.0 copy-start.2
  17.2 6.3 %copy.39 = bf16[1,2,2048,448]{3,2,1,0:T(8,128)(2,1)} copy(bf16[1,2,2048,448]{2,3,1,0:T(8,128)(2,1)} %param.21) | data formatting | bytes 7340032 | tf_op args[9]
  23.5 0.0 copy-done.2
  23.5 0.0 copy-start.4
  23.5 0.0 copy-start.5
  23.5 1.3 copy.36
  24.8 0.0 copy-done.4
  24.8 0.6 broadcast_in_dim_squeeze.9.in_row_ids
  25.4 1.0 copy.40.in_col_ids
  26.4 0.0 copy-done.5
  26.4 1.0 copy.41.target_col_ids
  27.4 11.2 %all-gather.5.cloned.1.call-done.down_hbm = bf16[448,2048]{1,0:T(8,128)(2,1)} async-done(((bf16[448,512]{1,0:T(8,128)(2,1)}), bf16[448,2048]{1,0:T(8,128)(2,1)}) %all-gather.5.cloned.1.call-update) | async-done | bytes 1835024 | tf_op jit(solution)/shard_map/all_gather | solution.py:523
  38.6 40.2 %all-gather.3.cloned.1.call-done.gu_hbm = bf16[2,2048,448]{2,1,0:T(8,128)(2,1)} async-done(((bf16[2,512,448]{2,1,0:T(8,128)(2,1)}), bf16[2,2048,448]{2,1,0:T(8,128)(2,1)}) %all-gather.3.cloned.1.call-update) | async-done | bytes 3670032 | tf_op jit(solution)/shard_map/all_gather | solution.py:522
  78.8 156.1 %inner_steps.1 = (bf16[2,2048,448]{2,1,0:T(8,128)(2,1)}, bf16[448,2048]{1,0:T(8,128)(2,1)}) custom-call(s32[4,1,256]{2,1,0:T(1,128)} %broadcast_in_dim_squeeze.9.in_row_ids, s32[4,256,1]{2,1,0:T(8,128)} %copy.40.in_col_ids, s32[4,256,1]{2,1,0:T(8,128)} %copy.41.target_col_ids, bf16[256,2048]{1,0:T(8,128)(2,1)} %bitcast.13, bf16[2048,256]{1,0:T(8,128)(2,1)} %bitcast.14, ...), custom_call_target="tpu_custom_call" | custom-call | tf_op jit(solution)/shard_map/inner_steps/pallas_call | solution.py:444
  234.9 0.0 reduce-scatter.5.cloned.1.call-update
  234.9 0.0 reduce-scatter.3.cloned.1.call-start
  235.0 0.5 reduce-scatter.3.cloned.1.call-update
  235.5 1.9 copy.44
  237.4 0.0 copy-start.3
  237.4 3.0 copy.43
  240.4 44.2 %reduce-scatter.5.cloned.1.call-done = bf16[448,512]{1,0:T(8,128)(2,1)} async-done(((bf16[448,2048]{1,0:T(8,128)(2,1)}), bf16[448,512]{1,0:T(8,128)(2,1)}) %reduce-scatter.5.cloned.1.call-update) | async-done | bytes 458768 | tf_op jit(solution)/shard_map/reduce_scatter | solution.py:537
  284.6 0.0 copy-done.3
  284.6 2.9 multiply_subtract_fusion.1
  287.4 50.6 %reduce-scatter.3.cloned.1.call-done = bf16[2,512,448]{2,1,0:T(8,128)(2,1)} async-done(((bf16[2,2048,448]{2,1,0:T(8,128)(2,1)}), bf16[2,512,448]{2,1,0:T(8,128)(2,1)}) %reduce-scatter.3.cloned.1.call-update) | async-done | bytes 917520 | tf_op jit(solution)/shard_map/reduce_scatter | solution.py:536
  338.1 4.6 %multiply_add_fusion = (f32[2,512,448]{2,1,0:T(8,128)}, f32[2,512,448]{2,1,0:T(8,128)}) fusion(f32[2,512,448]{2,1,0:T(8,128)} %copy.43, bf16[2,512,448]{2,1,0:T(8,128)(2,1)} %reduce-scatter.3.cloned.1.call-done, f32[2,512,448]{2,1,0:T(8,128)S(1)} %copy.44), kind=kLoop, calls=%fused_computation.1 | loop fusion | flops 3670016 | bytes 8257536 | tf_op jit(solution)/shard_map/add | solution.py:541
  342.7 0.0 copy-start
  342.7 2.9 copy.45
  345.6 0.0 copy-done
  345.7 1.7 copy.46
Async XLA Ops:
  7.2 2.3 copy-start.1
  7.2 31.5 %all-gather.5.cloned.1.call-start = ((), (), s32[]{:S(2)}) async-start(), calls=%async_computation.3 | async-start | bytes 2293760 | tf_op jit(solution)/shard_map/all_gather | solution.py:523
  9.4 69.4 %all-gather.3.cloned.1.call-start = ((), (), s32[]{:S(2)}) async-start(), calls=%async_computation.2 | async-start | bytes 5242880 | tf_op jit(solution)/shard_map/all_gather | solution.py:522
  10.9 273.7 %reduce-scatter.5.cloned.1.call-start = ((), (), s32[]{:S(2)}) async-start(), calls=%async_computation.5 | async-start | bytes 2293760 | tf_op jit(solution)/shard_map/reduce_scatter | solution.py:537
  17.2 6.3 %copy-start.2 = (bf16[1,256,2048]{2,1,0:T(8,128)(2,1)S(1)}, bf16[1,256,2048]{2,1,0:T(8,128)(2,1)}, u32[]{:S(2)}) copy-start(bf16[1,256,2048]{2,1,0:T(8,128)(2,1)} %param.12) | copy-start | bytes 3145732
  23.5 1.3 copy-start.4
  23.5 2.9 copy-start.5
  234.9 103.1 %reduce-scatter.3.cloned.1.call-start = ((), (), s32[]{:S(2)}) async-start(), calls=%async_computation.4 | async-start | bytes 5242880 | tf_op jit(solution)/shard_map/reduce_scatter | solution.py:536
  237.4 47.2 %copy-start.3 = (f32[448,512]{1,0:T(8,128)S(1)}, f32[448,512]{1,0:T(8,128)}, u32[]{:S(2)}) copy-start(f32[448,512]{1,0:T(8,128)} %param.17) | copy-start | bytes 2752516
  342.7 3.0 copy-start
Sparse Core Ops, SparseCore 0:
  9.7 28.9 all-gather.4
  40.9 37.8 all-gather.2
  235.1 49.4 reduce-scatter.4
  287.3 50.7 reduce-scatter.2

commit v2 on v0

v2 whole, which is shorter than its diff:
```python
import math

import jax
import jax.numpy as jnp
from jax import lax
from jax.experimental import pallas as pl
from jax.experimental.pallas import tpu as pltpu
from jax.sharding import PartitionSpec as P

D = 2048
FF = 14336
STEPS = 4
TOK = 256
ROWS = 256
SHARDS = 32
HID = FF // SHARDS
SIDE = 4
REPS = 4
BW = D // REPS
BAND = TOK // SIDE
OWN = BAND // SIDE
HALF = BW // 2
THIN = HALF // 2
CUTS = 4
CUT = HID // CUTS
IN_FLIGHT = 3

beta_one = 0.9
beta_two = 0.95
inner_rate = 0.03
decay_rate = 0.1
epsilon = 1e-08
outer_rate = 0.7
momentum_rate = 0.9

in_scale = 1.0 / D**0.5
out_scale = 1.0 / FF**0.5
first_gain = inner_rate
step_gain = first_gain * (1.0 - beta_one)
second_gain = step_gain**2 / (1.0 - beta_two)
root_gain = math.sqrt(second_gain)
keep_rate = 1.0 - inner_rate * decay_rate

MESH = pl.DeviceIdType.MESH
VMEM = pltpu.VMEM
F32 = jnp.float32
BF16 = jnp.bfloat16


def adam(weight, grad, first, second, gain):
    t = grad * gain
    first = beta_one * first + t
    second = beta_two * second + t * t
    root = second * lax.rsqrt(second) + epsilon * root_gain
    move = first * pl.reciprocal(root, approx=True)
    return keep_rate * weight - root_gain * move, first, second


def dot(a, b):
    return jnp.dot(a, b, preferred_element_type=F32)


def dot_last(a, b):
    return lax.dot_general(a, b, (((1,), (1,)), ((), ())), preferred_element_type=F32)


def round_kernel(
    in_ids,
    target_ids,
    table_hbm,
    targets_hbm,
    outer_gu,
    outer_down,
    m_gu,
    v_gu,
    m_down,
    v_down,
    mom_gu,
    mom_down,
    new_gu,
    new_down,
    new_mom_gu,
    new_mom_down,
    table,
    targets,
    weight,
    first,
    second,
    start,
    narrow,
    stage,
    inputs,
    pick,
    wanted,
    gate_up_buf,
    slope_buf,
    silu_buf,
    hidden_grad,
    hidden_t,
    hidden,
    pre_grad,
    partial,
    land_one,
    sum_one,
    land_two,
    out_grad,
    land_mate,
    land_far,
    table_sem,
    load_sem,
    stage_sem,
    send_sem,
    recv_sem,
    z_send,
    z_recv,
    core_send,
    core_recv,
    fwd_send,
    fwd_recv,
    mate_send,
    mate_recv,
    far_send,
    far_recv,
    outer_sem,
    out_sem,
):
    rep = lax.axis_index("rep")
    fsdp = lax.axis_index("fsdp")
    zh, core = rep // 2, rep % 2
    zl = fsdp // (SIDE * SIDE)
    side = ((fsdp // SIDE) % SIDE, fsdp % SIDE)
    mate = (zh * 2 + (1 - core), fsdp)
    far = ((1 - zh) * 2 + core, fsdp)

    def quarter(n):
        return ((zh + n // 2) % 2) * 2 + (core + n % 2) % 2

    def cols_of(n):
        return pl.ds(pl.multiple_of(quarter(n) * BW, BW), BW)

    def peer(part, d_first, d_second, d_z):
        one = (side[part] + d_first) % SIDE
        two = (side[1 - part] + d_second) % SIDE
        z = (zl + d_z) % 2
        x, y = (one, two) if part == 0 else (two, one)
        return (rep, z * SIDE * SIDE + x * SIDE + y)

    cross = [(2, 1), (1, 1), (3, 1), (2, 0), (1, 0), (3, 0), (0, 1)]
    along = (2, 1, 3)
    partners = [mate, far]
    partners += [peer(0, o, 0, dz) for o in range(1, SIDE) for dz in range(2)]
    partners += [peer(0, 0, ds, dz) for ds, dz in cross]

    barrier = pltpu.get_barrier_semaphore()
    for other in partners:
        pl.semaphore_signal(barrier, inc=1, device_id=other, device_id_type=MESH)

    def in_rows(count, height, body, unroll=1):
        def go(i, carry):
            body(pl.ds(pl.multiple_of(i * height, height), height))
            return carry

        lax.fori_loop(0, count // height, go, 0, unroll=unroll)

    def remote(src, dst, one, two, other):
        return pltpu.make_async_remote_copy(
            src_ref=src,
            dst_ref=dst,
            send_sem=one,
            recv_sem=two,
            device_id=other,
            device_id_type=MESH,
        )

    def outer_cut(j, c):
        rows = pl.ds(c * CUT, CUT)
        source = outer_gu.at[j] if j < 2 else outer_down
        return pltpu.make_async_copy(
            source.at[rows, :], weight.at[0, j, rows, :], load_sem.at[j, c]
        )

    for j in range(3):
        for c in range(CUTS):
            outer_cut(j, c).start()
    tables = [
        pltpu.make_async_copy(source, held, table_sem.at[i])
        for i, (source, held) in enumerate(((table_hbm, table), (targets_hbm, targets)))
    ]
    for copy in tables:
        copy.start()
    blocks = [(j, n) for j in range(3) for n in range(REPS)]

    def moment_copies(i):
        j, n = blocks[i]
        sources = (m_gu.at[j], v_gu.at[j]) if j < 2 else (m_down, v_down)
        return [
            pltpu.make_async_copy(
                source.at[:, cols_of(n)], stage.at[i % 2, s], stage_sem.at[i % 2, s]
            )
            for s, source in enumerate(sources)
        ]

    for i in range(2):
        for copy in moment_copies(i):
            copy.start()

    def narrow_outer(j, c):
        outer_cut(j, c).wait()
        for r in range(0, CUT, 16):
            rows = pl.ds(c * CUT + r, 16)
            start[0, j, rows, :] = weight[0, j, rows, :].astype(BF16)

    narrow_outer(0, 0)
    pl.semaphore_wait(barrier, len(partners))

    cuts = [(j, c) for j in range(3) for c in range(CUTS)]

    def z_copy(i):
        j, c = cuts[i]
        rows = pl.ds(c * CUT, CUT)
        return remote(
            start.at[0, j, rows, :], start.at[2, j, rows, :], z_send.at[i], z_recv.at[i], far
        )

    def fwd_copy(i):
        j, c = cuts[i]
        rows = pl.ds(c * CUT, CUT)
        return remote(
            start.at[2, j, rows, :], start.at[3, j, rows, :], fwd_send.at[i], fwd_recv.at[i], mate
        )

    def core_copy(j):
        return remote(start.at[0, j], start.at[1, j], core_send.at[j], core_recv.at[j], mate)

    for j, c in cuts:
        if (j, c) != (0, 0):
            narrow_outer(j, c)
        if j * CUTS + c < IN_FLIGHT:
            z_copy(j * CUTS + c).start()
        if c == CUTS - 1:
            core_copy(j).start()

    def widen(j, n):
        def rows_of(rows):
            weight[n, j, rows, :] = start[n, j, rows, :].astype(F32)

        in_rows(HID, 16, rows_of, 2)

    def take_moments(i):
        j, n = blocks[i]
        for copy in moment_copies(i):
            copy.wait()

        def rows_of(rows):
            first[n, j, rows, :] = stage[i % 2, 0, rows, :].astype(F32) * first_gain
            second[n, j, rows, :] = stage[i % 2, 1, rows, :].astype(F32) * second_gain

        in_rows(HID, 16, rows_of, 2)
        if i + 2 < len(blocks):
            for copy in moment_copies(i + 2):
                copy.start()

    def take_cut(i):
        copy = z_copy(i)
        copy.wait_recv()
        fwd_copy(i).start()
        copy.wait_send()
        if i + IN_FLIGHT < len(cuts):
            z_copy(i + IN_FLIGHT).start()

    def chosen_t(ids, k):
        rows = lax.broadcasted_iota(jnp.int32, (ROWS, TOK), 0)
        return (ids[pl.ds(k, 1), :] == rows).astype(F32)

    def look_up_inputs(k, slot):
        chosen = chosen_t(in_ids, k).T.astype(BF16)
        for n in range(REPS):
            inputs[slot, n] = dot(chosen, table[:, cols_of(n)]).astype(BF16)

    def band(coordinate):
        return pl.ds(pl.multiple_of(coordinate * BAND, BAND), BAND)

    def own_rows(one, two):
        return pl.ds(pl.multiple_of(one * BAND + two * OWN, OWN), OWN)

    def thin_cols(base, z):
        return pl.ds(pl.multiple_of(base + z * THIN, THIN), THIN)

    def send(kind, n, h, src, dst, other):
        remote(src, dst, send_sem.at[kind, n, h], recv_sem.at[kind, n, h], other).start()

    def wait_bytes(kind, n, h, sem):
        like = land_one.at[n, h] if kind in (0, 3) else land_two.at[n, h]
        pltpu.make_async_copy(like, like, sem.at[kind, n, h]).wait()

    def scatter_one(n, held):
        partial[n] = (dot(hidden[...], held[n, 2]) * out_scale).astype(BF16)
        for h in range(2):
            cols = pl.ds(h * HALF, HALF)
            for o in along:
                src = partial.at[n, band((side[h] + o) % SIDE), cols]
                send(0, n, h, src, land_one.at[n, h, o - 1], peer(h, o, 0, 0))

    def scatter_two(n):
        for h in range(2):
            wait_bytes(0, n, h, recv_sem)
            total = partial[n, band(side[h]), pl.ds(h * HALF, HALF)].astype(F32)
            for o in range(SIDE - 1):
                total = total + land_one[n, h, o].astype(F32)
            sum_one[n, h] = total.astype(BF16)
            for i, (ds, dz) in enumerate(cross):
                to = (side[1 - h] + ds) % SIDE
                rows = pl.ds(pl.multiple_of(to * OWN, OWN), OWN)
                src = sum_one.at[n, h, rows, thin_cols(0, (zl + dz) % 2)]
                send(1, n, h, src, land_two.at[n, h, i], peer(h, 0, ds, dz))

    def gather_one(n):
        for h in range(2):
            wait_bytes(1, n, h, recv_sem)
            rows = pl.ds(pl.multiple_of(side[1 - h] * OWN, OWN), OWN)
            total = sum_one[n, h, rows, thin_cols(0, zl)].astype(F32)
            for i in range(len(cross)):
                total = total + land_two[n, h, i].astype(F32)
            mine = (n, own_rows(side[h], side[1 - h]), thin_cols(h * HALF, zl))
            out_grad[mine] = ((total - wanted[n, h]) * (1.0 / TOK)).astype(BF16)
            for ds, dz in cross:
                send(2, n, h, out_grad.at[mine], out_grad.at[mine], peer(h, 0, ds, dz))

    def gather_two(n):
        for h in range(2):
            wait_bytes(2, n, h, recv_sem)
            mine = out_grad.at[n, band(side[h]), pl.ds(h * HALF, HALF)]
            for o in along:
                send(3, n, h, mine, mine, peer(h, o, 0, 0))

    def update(n, j, product, last):
        gain = step_gain * (in_scale if j < 2 else out_scale)
        for r in range(0, HID, 16):
            here = (n, j, pl.ds(r, 16), slice(None))
            w, m, v = adam(weight[here], product[r : r + 16, :], first[here], second[here], gain)
            if last:
                narrow[here] = (start[here].astype(F32) - w).astype(BF16)
            else:
                weight[here] = w
                first[here] = m
                second[here] = v
                narrow[here] = w.astype(BF16)

    def use_block(n, held, fresh):
        for h in range(2):
            wait_bytes(3, n, h, recv_sem)
        product = dot_last(held[n, 2], out_grad[n])
        if fresh:
            hidden_grad[...] = product
        else:
            hidden_grad[...] += product

    def update_down(n, slot, last):
        update(n, 2, dot(hidden_t[slot], out_grad[n]), last)

    def update_gu(n, slot, last):
        product = dot(pre_grad[...], inputs[slot, n])
        for j in range(2):
            update(n, j, product[j * HID : (j + 1) * HID, :], last)

    def update_all_gu(slot):
        for n in range(REPS):
            update_gu(n, slot, False)

    def update_late(slot):
        for n in range(2):
            update_down(n, slot, False)

    def forward(held, slot):
        both = [held[n, 0:2].reshape(2 * HID, BW) for n in range(REPS)]
        rows_in = jnp.concatenate([inputs[slot, n] for n in range(REPS)], axis=1)
        gate_up_buf[...] = dot_last(jnp.concatenate(both, axis=1), rows_in)
        for r in range(0, HID, 16):
            rows = pl.ds(r, 16)
            gate = gate_up_buf[rows, :] * in_scale
            upper = gate_up_buf[pl.ds(HID + r, 16), :] * in_scale
            sigmoid = jax.nn.sigmoid(gate)
            silu = gate * sigmoid
            hidden_t[slot, rows, :] = (silu * upper).astype(BF16)
            silu_buf[rows, :] = silu * out_scale
            slope_buf[rows, :] = upper * sigmoid * (1.0 + gate * (1.0 - sigmoid)) * out_scale
        hidden[...] = hidden_t[slot].T

    def look_up_targets(k):
        pick[...] = chosen_t(target_ids, k).T.astype(BF16)
        for n in range(REPS):
            for h in range(2):
                rows = own_rows(side[h], side[1 - h])
                cols = thin_cols(quarter(n) * BW + h * HALF, zl)
                wanted[n, h] = dot(pick[rows, :], targets[:, cols])

    def backward():
        pre_grad[:HID, :] = (hidden_grad[...] * slope_buf[...]).astype(BF16)
        pre_grad[HID:, :] = (hidden_grad[...] * silu_buf[...]).astype(BF16)

    def end_sends():
        for n in range(REPS):
            for kind in range(4):
                for h in range(2):
                    wait_bytes(kind, n, h, send_sem)

    for copy in tables:
        copy.wait()
    look_up_inputs(0, 0)
    for j in range(3):
        widen(j, 0)
    for i in range(2 * CUTS):
        take_moments(i)
        take_cut(i)
    for j in range(2):
        core_copy(j).wait_recv()
        widen(j, 1)
    for i in range(2 * CUTS):
        fwd_copy(i).wait_recv()
    forward(start, 0)
    core_copy(2).wait_recv()
    scatter_one(0, start)
    scatter_one(1, start)
    look_up_targets(0)
    take_cut(8)
    take_moments(8)
    scatter_two(0)
    scatter_two(1)
    take_cut(9)
    widen(2, 1)
    gather_one(0)
    gather_one(1)
    take_cut(10)
    take_moments(9)
    gather_two(0)
    gather_two(1)
    take_cut(11)
    for i in range(2 * CUTS, 3 * CUTS):
        fwd_copy(i).wait_recv()
    scatter_one(2, start)
    scatter_one(3, start)
    take_moments(10)
    take_moments(11)
    use_block(0, start, True)
    scatter_two(2)
    scatter_two(3)
    use_block(1, start, False)
    look_up_inputs(1, 1)
    gather_one(2)
    gather_one(3)
    for j in range(3):
        widen(j, 2)
        widen(j, 3)
    gather_two(2)
    gather_two(3)
    for n in (2, 3):
        use_block(n, start, False)
        update_down(n, 0, False)
    backward()
    update_all_gu(0)
    end_sends()

    def middle(k, slot, order, last):
        a, b, c, d = order
        forward(narrow, slot)
        scatter_one(a, narrow)
        scatter_one(b, narrow)
        update_late(1 - slot)
        if last:
            look_up_targets(k)
            for n in (a, b):
                scatter_two(n)
            for n in (c, d):
                scatter_one(n, narrow)
            for n in (a, b):
                gather_one(n)
            for n in (c, d):
                scatter_two(n)
            for n in (a, b):
                gather_two(n)
            for n in (c, d):
                gather_one(n)
            use_block(a, narrow, True)
            update_down(a, slot, True)
            return
        scatter_one(c, narrow)
        scatter_one(d, narrow)
        look_up_targets(k)
        look_up_inputs(k + 1, 1 - slot)
        for stage_of in (scatter_two, gather_one, gather_two):
            for n in order:
                stage_of(n)
        use_block(a, narrow, True)
        update_down(a, slot, False)

    def step(k, carry):
        slot = k % 2
        middle(k, slot, (2, 3, 0, 1), False)
        use_block(3, narrow, False)
        update_down(3, slot, False)
        use_block(0, narrow, False)
        use_block(1, narrow, False)
        backward()
        update_all_gu(slot)
        end_sends()
        return carry

    lax.fori_loop(1, STEPS - 1, step, 0)

    def mate_copy(j, n):
        return remote(
            narrow.at[n, j],
            land_mate.at[j, n // 2],
            mate_send.at[j, n // 2],
            mate_recv.at[j, n // 2],
            mate,
        )

    def far_copy(j, c):
        rows = pl.ds(c * CUT, CUT)
        return remote(
            narrow.at[2, j, rows, :], land_far.at[j, rows, :], far_send.at[j, c], far_recv.at[j, c], far
        )

    def pair_sum(j):
        mate_copy(j, 3).wait_recv()
        for c in range(CUTS):
            def rows_of(r):
                rows = pl.ds(pl.multiple_of(c * CUT + r * 16, 16), 16)
                both = narrow[2, j, rows, :].astype(F32) + land_mate[j, 1, rows, :].astype(F32)
                narrow[2, j, rows, :] = both.astype(BF16)

            for r in range(CUT // 16):
                rows_of(r)
            far_copy(j, c).start()

    outer_loads = [
        pltpu.make_async_copy(source.at[j] if j < 2 else flat, held.at[3, j], outer_sem.at[i, j])
        for i, (source, flat, held) in enumerate(
            ((outer_gu, outer_down, first), (mom_gu, mom_down, second))
        )
        for j in range(3)
    ]
    slot = (STEPS - 1) % 2
    middle(STEPS - 1, slot, (3, 2, 0, 1), True)
    mate_copy(2, 3).start()
    use_block(2, narrow, False)
    update_down(2, slot, True)
    gather_two(0)
    gather_two(1)
    pair_sum(2)
    use_block(0, narrow, False)
    use_block(1, narrow, False)
    backward()
    update_gu(3, slot, True)
    for j in range(2):
        mate_copy(j, 3).start()
    for copy in outer_loads:
        copy.start()
    update_gu(2, slot, True)
    for j in range(2):
        pair_sum(j)
    update_down(1, slot, True)
    mate_copy(2, 1).start()
    update_gu(1, slot, True)
    for j in range(2):
        mate_copy(j, 1).start()
    update_down(0, slot, True)
    update_gu(0, slot, True)
    end_sends()

    def out_copies(j, c):
        rows = pl.ds(c * CUT, CUT)
        outs = (new_gu.at[j], new_mom_gu.at[j]) if j < 2 else (new_down, new_mom_down)
        return [
            pltpu.make_async_copy(
                weight.at[i, j, rows, :], out.at[rows, :], out_sem.at[j, c, i]
            )
            for i, out in enumerate(outs)
        ]

    for copy in outer_loads:
        copy.wait()
    for j in (2, 0, 1):
        mate_copy(j, 1).wait_recv()
        for c in range(CUTS):
            far_copy(j, c).wait_recv()
            for r in range(CUT // 16):
                rows = pl.ds(c * CUT + r * 16, 16)
                total = (
                    narrow[0, j, rows, :].astype(F32)
                    + land_mate[j, 0, rows, :].astype(F32)
                    + land_far[j, rows, :].astype(F32)
                )
                mean = total / REPS
                new_mom = momentum_rate * second[3, j, rows, :] + mean
                weight[1, j, rows, :] = new_mom
                weight[0, j, rows, :] = first[3, j, rows, :] - outer_rate * (
                    mean + momentum_rate * new_mom
                )
            for copy in out_copies(j, c):
                copy.start()

    for j in range(3):
        core_copy(j).wait_send()
        for n in (1, 3):
            mate_copy(j, n).wait_send()
        for c in range(CUTS):
            far_copy(j, c).wait_send()
            for copy in out_copies(j, c):
                copy.wait()
    for i in range(len(cuts)):
        fwd_copy(i).wait_send()


def whole_round(in_ids, target_ids, table, targets, outer_gu, outer_down, *moments):
    in_vmem = pl.BlockSpec(memory_space=VMEM)
    anywhere = pl.BlockSpec(memory_space=pl.ANY)
    every = (REPS, 3, HID, BW)
    dma = pltpu.SemaphoreType.DMA
    gu_shape = jax.ShapeDtypeStruct((2, HID, BW), F32)
    down_shape = jax.ShapeDtypeStruct((HID, BW), F32)
    return pl.pallas_call(
        round_kernel,
        out_shape=(gu_shape, down_shape, gu_shape, down_shape),
        in_specs=[in_vmem] * 2 + [anywhere] * 10,
        out_specs=(anywhere,) * 4,
        scratch_shapes=[
            VMEM((ROWS, D), BF16),
            VMEM((ROWS, D), BF16),
            VMEM(every, F32),
            VMEM(every, F32),
            VMEM(every, F32),
            VMEM(every, BF16),
            VMEM(every, BF16),
            VMEM((2, 2, HID, BW), BF16),
            VMEM((2, REPS, TOK, BW), BF16),
            VMEM((TOK, ROWS), BF16),
            VMEM((REPS, 2, OWN, THIN), F32),
            VMEM((2 * HID, TOK), F32),
            VMEM((HID, TOK), F32),
            VMEM((HID, TOK), F32),
            VMEM((HID, TOK), F32),
            VMEM((2, HID, TOK), BF16),
            VMEM((TOK, HID), BF16),
            VMEM((2 * HID, TOK), BF16),
            VMEM((REPS, TOK, BW), BF16),
            VMEM((REPS, 2, SIDE - 1, BAND, HALF), BF16),
            VMEM((REPS, 2, BAND, HALF), BF16),
            VMEM((REPS, 2, 2 * SIDE - 1, OWN, THIN), BF16),
            VMEM((REPS, TOK, BW), BF16),
            VMEM((3, 2, HID, BW), BF16),
            VMEM((3, HID, BW), BF16),
            dma((2,)),
            dma((3, CUTS)),
            dma((2, 2)),
            dma((4, REPS, 2)),
            dma((4, REPS, 2)),
            dma((3 * CUTS,)),
            dma((3 * CUTS,)),
            dma((3,)),
            dma((3,)),
            dma((3 * CUTS,)),
            dma((3 * CUTS,)),
            dma((3, 2)),
            dma((3, 2)),
            dma((3, CUTS)),
            dma((3, CUTS)),
            dma((2, 3)),
            dma((3, CUTS, 2)),
        ],
        compiler_params=pltpu.CompilerParams(
            collective_id=0, has_side_effects=True, vmem_limit_bytes=63 * 2**20
        ),
        name="inner_round",
    )(in_ids, target_ids, table, targets, outer_gu, outer_down, *moments)


def hand_over_kernel(*refs):
    sources, results, (held, in_sem, out_sem) = refs[:4], refs[4:8], refs[8:]
    ins, outs = [], []
    for i in range(6):
        n, j = (i // 2 * 2, i % 2) if i < 4 else ((i - 4) * 2 + 1, None)
        source = sources[n] if j is None else sources[n].at[j]
        result = results[n] if j is None else results[n].at[j]
        ins.append(pltpu.make_async_copy(source, held.at[i], in_sem.at[i]))
        outs.append(pltpu.make_async_copy(held.at[i], result, out_sem.at[i]))
    for copy in ins:
        copy.start()
    for one, two in zip(ins, outs):
        one.wait()
        two.start()
    for copy in outs:
        copy.wait()


def hand_over(*arrays):
    anywhere = pl.BlockSpec(memory_space=pl.ANY)
    return pl.pallas_call(
        hand_over_kernel,
        out_shape=tuple(jax.ShapeDtypeStruct(array.shape, F32) for array in arrays),
        in_specs=[anywhere] * 4,
        out_specs=(anywhere,) * 4,
        scratch_shapes=[
            VMEM((6, HID, BW), F32),
            pltpu.SemaphoreType.DMA((6,)),
            pltpu.SemaphoreType.DMA((6,)),
        ],
        name="hand_over",
    )(*arrays)


def on_device(
    in_table,
    target_table,
    in_ids,
    target_ids,
    gate_up,
    down,
    mom_gate_up,
    mom_down,
    m_gate_up,
    v_gate_up,
    m_down,
    v_down,
):
    news = whole_round(
        in_ids[0],
        target_ids[0],
        in_table[0],
        target_table[0],
        jnp.swapaxes(gate_up, 1, 2),
        down,
        jnp.swapaxes(m_gate_up[0], 1, 2),
        jnp.swapaxes(v_gate_up[0], 1, 2),
        m_down[0],
        v_down[0],
        jnp.swapaxes(mom_gate_up, 1, 2),
        mom_down,
    )
    new_gu, new_down, new_mom_gu, new_mom_down = hand_over(*news)
    return (jnp.swapaxes(new_gu, 1, 2), new_down, jnp.swapaxes(new_mom_gu, 1, 2), new_mom_down)


def solution(mesh):
    in_specs = (
        P("rep", None, None),
        P("rep", None, None),
        P("rep", None, None),
        P("rep", None, None),
        P(None, "rep", "fsdp"),
        P("fsdp", "rep"),
        P(None, "rep", "fsdp"),
        P("fsdp", "rep"),
        P("rep", None, None, "fsdp"),
        P("rep", None, None, "fsdp"),
        P("rep", "fsdp", None),
        P("rep", "fsdp", None),
    )
    out_specs = (P(None, "rep", "fsdp"), P("fsdp", "rep"), P(None, "rep", "fsdp"), P("fsdp", "rep"))
    return jax.shard_map(
        on_device, mesh=mesh, in_specs=in_specs, out_specs=out_specs, check_vma=False
    )
```

time: 1570 us -> 183 us (0.12)
  waiting for transfers between devices: 1380 us -> 0 us
  Pallas kernels: 0 us -> 182 us
  matrix products: 121 us -> 0 us
  local copies, waits for them, and re-layouts: 29.1 us -> 0 us
  other arithmetic: 17.7 us -> 0 us
    reduce_scatter x6 -> x0, waiting for transfers between devices: 699 us -> none  [the longest x4 613 us: on_device(): lax.psum_scatter(jnp.dot(hidden, down_b, preferred_element_type=jnp.float...]
    all_gather x6 -> x0, waiting for transfers between devices: 685 us -> none  [the longest x4 596 us: on_device(): out_grad = lax.all_gather(own_grad, 'fsdp', axis=0, tiled=True)]
    pallas_call x0 -> x2, Pallas kernels: none -> 182 us  [the longest x1 178 us: whole_round(): pl.pallas_call(round_kernel, out_shape=(gu_shape, down_shape, gu_shape, d...]
    dot_general x24 -> x0, matrix products: 121 us -> none  [the longest x4 62.6 us: on_device(): jnp.einsum('td,ktf->kdf', inputs, pre_grad, preferred_element_type=jnp.fl...]
  transfers between devices with their start and end apart: 12 -> 0, of which waited for: 12 -> 0; matrix products, arithmetic and copies ran while one was open for 3% -> 0% of each run, Pallas kernels for 0% -> 0%
where the time goes in v2:
time: 183 us
  Pallas kernels  182 us (99%)
    pallas_call x1, Pallas kernels, whole_round(): pl.pallas_call(round_kernel, out_shape=(gu_shape, down_shape, gu_shape, d...  178 us
    pallas_call x1, Pallas kernels, hand_over(): pl.pallas_call(hand_over_kernel, out_shape=tuple((jax.ShapeDtypeStruct(ar...  4.73 us

profile of v2, /device:TPU:1, one launch (start us, length us, event | category | flops | bytes accessed | tf_op | source)
XLA Modules:
  0.0 183.2 jit_solution(9746959449967610371)
XLA Ops:
  0.6 177.6 %inner_round.1 = (f32[2,448,512]{2,1,0:T(8,128)}, f32[448,512]{1,0:T(8,128)}, f32[2,448,512]{2,1,0:T(8,128)}, f32[448,512]{1,0:T(8,128)}) custom-call(s32[4,256]{1,0:T(4,128)} %bitcast.24, s32[4,256]{1,0:T(4,128)} %bitcast.25, bf16[256,2048]{1,0:T(8,128)(2,1)} %bitcast.22, bf16[256,2048]{1,0:T(8,128)(2,1)} %bitcast.23, f32[2,448,512]{2,1,0:T(8,128)} %bitcast.18, ...), custom_call_target="tpu_custom_call" | custom-call | tf_op jit(solution)/shard_map/inner_round/pallas_call | solution.py:623
  178.3 4.7 %hand_over.1 = (f32[2,448,512]{2,1,0:T(8,128)}, f32[448,512]{1,0:T(8,128)}, f32[2,448,512]{2,1,0:T(8,128)}, f32[448,512]{1,0:T(8,128)}) custom-call(f32[2,448,512]{2,1,0:T(8,128)} %get-tuple-element.12.refs_0_, f32[448,512]{1,0:T(8,128)} %get-tuple-element.13.refs_1_, f32[2,448,512]{2,1,0:T(8,128)} %get-tuple-element.14.refs_2_, ...), custom_call_target="tpu_custom_call" | custom-call | tf_op jit(solution)/shard_map/hand_over/pallas_call | solution.py:699

commit v3 on v2

--- a/solution.py
+++ b/solution.py
@@ -432,8 +432,6 @@
     gather_one(1)
     take_cut(10)
     take_moments(9)
-    gather_two(0)
-    gather_two(1)
     take_cut(11)
     for i in range(2 * CUTS, 3 * CUTS):
         fwd_copy(i).wait_recv()
@@ -441,16 +439,20 @@
     scatter_one(3, start)
     take_moments(10)
     take_moments(11)
-    use_block(0, start, True)
+    look_up_inputs(1, 1)
     scatter_two(2)
     scatter_two(3)
-    use_block(1, start, False)
-    look_up_inputs(1, 1)
+    gather_two(0)
+    gather_two(1)
+    for j in range(2):
+        widen(j, 2)
+        widen(j, 3)
     gather_one(2)
     gather_one(3)
-    for j in range(3):
-        widen(j, 2)
-        widen(j, 3)
+    widen(2, 2)
+    widen(2, 3)
+    use_block(0, start, True)
+    use_block(1, start, False)
     gather_two(2)
     gather_two(3)
     for n in (2, 3):

time: 183 us -> 181 us (0.989)
  Pallas kernels: 182 us -> 180 us
    pallas_call x1, Pallas kernels: 178 us -> 175 us  [whole_round(): pl.pallas_call(round_kernel, out_shape=(gu_shape, down_shape, gu_shape, d...]
where the time goes in v3:
time: 181 us; the launch traced here: 180 us
  Pallas kernels  180 us (99%)
    pallas_call x1, Pallas kernels, whole_round(): pl.pallas_call(round_kernel, out_shape=(gu_shape, down_shape, gu_shape, d...  175 us
    pallas_call x1, Pallas kernels, hand_over(): pl.pallas_call(hand_over_kernel, out_shape=tuple((jax.ShapeDtypeStruct(ar...  4.73 us

profile of v3, /device:TPU:1, one launch (start us, length us, event | category | flops | bytes accessed | tf_op | source)
XLA Modules:
  0.0 180.4 jit_solution(5993472917792441310)
XLA Ops:
  0.6 174.8 %inner_round.1 = (f32[2,448,512]{2,1,0:T(8,128)}, f32[448,512]{1,0:T(8,128)}, f32[2,448,512]{2,1,0:T(8,128)}, f32[448,512]{1,0:T(8,128)}) custom-call(s32[4,256]{1,0:T(4,128)} %bitcast.24, s32[4,256]{1,0:T(4,128)} %bitcast.25, bf16[256,2048]{1,0:T(8,128)(2,1)} %bitcast.22, bf16[256,2048]{1,0:T(8,128)(2,1)} %bitcast.23, f32[2,448,512]{2,1,0:T(8,128)} %bitcast.18, ...), custom_call_target="tpu_custom_call" | custom-call | tf_op jit(solution)/shard_map/inner_round/pallas_call | solution.py:625
  175.5 4.7 %hand_over.1 = (f32[2,448,512]{2,1,0:T(8,128)}, f32[448,512]{1,0:T(8,128)}, f32[2,448,512]{2,1,0:T(8,128)}, f32[448,512]{1,0:T(8,128)}) custom-call(f32[2,448,512]{2,1,0:T(8,128)} %get-tuple-element.12.refs_0_, f32[448,512]{1,0:T(8,128)} %get-tuple-element.13.refs_1_, f32[2,448,512]{2,1,0:T(8,128)} %get-tuple-element.14.refs_2_, ...), custom_call_target="tpu_custom_call" | custom-call | tf_op jit(solution)/shard_map/hand_over/pallas_call | solution.py:701
